TPU v7x, 32 devices: a whole 2x2x4 slice. The times are simulated.
32 devices in a mesh: dp: 8 (over z, core), expert: 4 (over y, x).
Axes of the slice: x: 2, y: 2, z: 4, core: 2. Of those that a mesh axis runs over, the one named last changes fastest.
Arguments:
- tokens: bfloat16 [8192, 2048], P(('dp', 'expert')), parts along dimension 0, may hold values from -6 to 6
- routes: int32 [8192, 2], P(('dp', 'expert')), parts along dimension 0, may hold values from 0 to 3, all different within a row; in each aligned block of 256 rows (0 to 255, 256 to 511, ...) at most 256 rows name the same one
- gate_values: bfloat16 [8192, 2], P(('dp', 'expert')), parts along dimension 0, may hold values from 0.099609375 to 1
- weight_in: bfloat16 [4, 2048, 1536], P('expert'), may hold values from -0.125 to 0.125
- weight_out: bfloat16 [4, 768, 2048], P('expert'), may hold values from -0.21875 to 0.21875
Outputs:
- mixed: bfloat16 [8192, 2048], P(('dp', 'expert')), parts along dimension 0
There are 8 independent parts, one for each index of `dp`. A program takes and returns all parts, laid end to end along the dimension named above; an argument that names none is the same for every part. Nothing has to cross between parts.
Inputs may be any that keep to these rules, and one draw needn't show every extreme that they name: `routes`: each row names 2 different experts. In each aligned block of 256 rows (the rows of one device) no expert is named by more than 256 rows, a bound that some block reaches.
All inputs are finite; a program needn't handle non-finite values.
Results may differ from a plain program's by a relative error of at most 0.012.
Values may be sent and summed in bfloat16 or wider, within the bound.
A program may use at most 128 MiB of HBM per device.

v0:
```python
from functools import partial

import jax
import jax.numpy as jnp
from jax import lax
from jax.sharding import PartitionSpec as P


def assign_slots(route_block, gate_block, expert_id, capacity):
    count_rows = route_block.shape[0]
    matched = route_block == expert_id
    chosen = jnp.any(matched, axis=1)
    weights = jnp.sum(jnp.where(matched, gate_block.astype(jnp.float32), 0.0), axis=1)
    position = jnp.cumsum(chosen.astype(jnp.int32)) - 1
    target = jnp.where(chosen, position, capacity)
    slot_rows = (
        jnp.full((capacity,), count_rows, jnp.int32)
        .at[target]
        .set(jnp.arange(count_rows, dtype=jnp.int32), mode="drop")
    )
    is_used = slot_rows < count_rows
    clipped = jnp.minimum(slot_rows, count_rows - 1)
    slot_weight = jnp.where(is_used, weights[clipped], 0.0)
    return (slot_rows, clipped, slot_weight)


def expert_block(gathered_rows, slot_weight, w_first, w_second):
    width = gathered_rows.shape[-1]
    hidden_units = w_second.shape[0]
    flat_rows = gathered_rows.reshape(-1, width)
    projected = jnp.dot(flat_rows, w_first, preferred_element_type=jnp.float32)
    hidden = (jax.nn.silu(projected[:, :hidden_units]) * projected[:, hidden_units:]).astype(
        jnp.bfloat16
    )
    expert_out = jnp.dot(hidden, w_second, preferred_element_type=jnp.float32)
    contribution = (expert_out * slot_weight.reshape(-1, 1)).astype(jnp.bfloat16)
    return contribution.reshape(gathered_rows.shape)


def local(tokens, routes, gate_values, weight_in, weight_out):
    groups = lax.axis_size("expert")
    tok_rows = tokens.shape[0]
    width = tokens.shape[1]
    capacity = min(tok_rows, 2 * tok_rows * routes.shape[1] // groups)
    w_first = weight_in[0]
    w_second = weight_out[0]
    gathered, gates_all, routes_all = (
        lax.all_gather(tokens, "expert", axis=0, tiled=True),
        lax.all_gather(gate_values, "expert", axis=0, tiled=True),
        lax.all_gather(routes, "expert", axis=0, tiled=True),
    )
    my_expert = lax.axis_index("expert")
    gathered = gathered.reshape(groups, tok_rows, width)
    slot_rows, clipped, slot_weight = jax.vmap(
        partial(assign_slots, expert_id=my_expert, capacity=capacity)
    )(routes_all.reshape(groups, tok_rows, -1), gates_all.reshape(groups, tok_rows, -1))
    picked = jnp.take_along_axis(gathered, clipped[:, :, None], axis=1)
    contribution = expert_block(picked, slot_weight, w_first, w_second)
    sources = jnp.broadcast_to(jnp.arange(groups, dtype=jnp.int32)[:, None], slot_rows.shape)
    partial_out = (
        jnp.zeros((groups, tok_rows, width), jnp.float32)
        .at[sources, slot_rows]
        .add(contribution.astype(jnp.float32), mode="drop")
    )
    summed = lax.psum_scatter(
        partial_out.reshape(groups * tok_rows, width).astype(jnp.bfloat16),
        "expert",
        scatter_dimension=0,
        tiled=True,
    )
    return summed


def solution(mesh):
    in_specs = (
        P(("dp", "expert"), None),
        P(("dp", "expert"), None),
        P(("dp", "expert"), None),
        P("expert", None, None),
        P("expert", None, None),
    )
    out_specs = P(("dp", "expert"), None)
    return jax.shard_map(local, mesh=mesh, in_specs=in_specs, out_specs=out_specs, check_vma=False)
```

profile of v0, /device:TPU:0, one launch (start us, length us, event | category | flops | bytes accessed | tf_op | source)
XLA Modules:
  0.0 212.8 jit_solution(1921740587040229112)
XLA Ops:
  6.5 0.0 copy-start
  6.5 0.0 all-gather.2.cloned.1.call-start
  6.5 0.7 all-gather.2.cloned.1.call-update
  7.3 0.0 reduce-scatter.2.cloned.1.call-start
  7.3 9.8 %all_gather.9 = s32[1024,2]{0,1:T(2,128)S(1)} all-gather(s32[256,2]{0,1:T(2,128)} %param.6), channel_id=1, replica_groups=mesh['dp'=8,'expert'=4] {'expert'}, dimensions={0}, use_global_device_ids=true | all-gather | bytes 10240 | tf_op jit(solution)/shard_map/all_gather | solution.py:50
  17.2 7.9 %all_gather.11 = bf16[1024,2]{0,1:T(2,128)(2,1)S(1)} all-gather(bf16[256,2]{0,1:T(2,128)(2,1)} %param.7), channel_id=1, replica_groups=mesh['dp'=8,'expert'=4] {'expert'}, dimensions={0}, use_global_device_ids=true | all-gather | bytes 5120 | tf_op jit(solution)/shard_map/all_gather | solution.py:49
  25.1 1.2 reduce-window.6
  26.3 0.1 slice.20
  26.4 0.1 copy.8
  26.6 0.1 copy.9
  26.7 0.1 add_add_fusion
  26.8 0.7 multiply_reduce_fusion.1
  27.5 0.7 and_reduce_fusion.1
  28.3 4.3 %scatter_custom_fusion = s32[1024]{0:T(1024)S(1)} fusion(s32[1024]{0:T(1024)S(1)} %bitcast.45, s32[1024]{0:T(1024)S(1)} %bitcast.42, s32[]{:T(128)} %constant.13.clone.1), kind=kCustom, calls=%fused_computation.35 | custom fusion | bytes 4100
  32.6 0.7 multiply_reduce_fusion
  33.3 0.7 and_reduce_fusion
  34.1 9.1 %gather_fusion.1 = f32[1024]{0:T(1024)S(1)} fusion(f32[4,256]{1,0:T(4,128)S(1)} %reduce_sum.12, s32[1024]{0:T(1024)S(1)} %bitcast.35), kind=kCustom, calls=%fused_computation.1 | custom fusion | bytes 16384 | tf_op jit(solution)/shard_map/vmap()/gather | solution.py:23
  43.3 21.4 %all-gather.2.cloned.1.call-done = bf16[1024,2048]{1,0:T(8,128)(2,1)} async-done(((bf16[256,2048]{1,0:T(8,128)(2,1)}), bf16[1024,2048]{1,0:T(8,128)(2,1)}) %all-gather.2.cloned.1.call-update) | async-done | bytes 4194320 | tf_op jit(solution)/shard_map/all_gather | solution.py:48
  64.7 38.5 %gather_fusion = bf16[1024,2048]{1,0:T(8,128)(2,1)} fusion(bf16[4,256,2048]{2,1,0:T(8,128)(2,1)} %bitcast.37, s32[1024]{0:T(1024)S(1)} %bitcast.36), kind=kCustom, calls=%fused_computation | custom fusion | bytes 8396800 | tf_op jit(solution)/shard_map/jit(take_along_axis)/gather | solution.py:57
  103.2 2.6 %broadcast_select_fusion = bf16[4,256,2048]{2,1,0:T(8,128)(2,1)S(1)} fusion(bf16[4,256,2048]{2,1,0:T(8,128)(2,1)} %bitcast.38, pred[4,256]{1,0:T(4,128)(4,1)S(1)} %compare_and_fusion), kind=kLoop, calls=%fused_computation.10 | loop fusion | flops 2097152 | bytes 8389632 | tf_op jit(solution)/shard_map/jit(take_along_axis)/select_n | solution.py:57
  105.8 8.8 %fusion.2 = f32[1024,1536]{1,0:T(8,128)S(1)} fusion(bf16[1024,2048]{1,0:T(8,128)(2,1)S(1)} %bitcast.39, bf16[1,2048,1536]{2,1,0:T(8,128)(2,1)} %param.8), kind=kOutput, calls=%fused_computation.7 | convolution fusion | flops 6442450944 | bytes 16777216 | tf_op jit(solution)/shard_map/dot_general | solution.py:31
  114.6 0.0 copy-done
  114.6 5.1 %multiply_convert_fusion = bf16[1024,2048]{1,0:T(8,128)(2,1)} fusion(f32[1024]{0:T(1024)S(1)} %bitcast.44, bf16[1,768,2048]{2,1,0:T(8,128)(2,1)S(1)} %copy-done, f32[1024,1536]{1,0:T(8,128)S(1)} %fusion.2), kind=kOutput, calls=%fused_computation.6 | convolution fusion | flops 3230138368 | bytes 13635584 | tf_op jit(solution)/shard_map/dot_general | solution.py:35
  119.7 18.5 %scatter_custom_fusion.1 = f32[1024,2048]{1,0:T(8,128)} fusion(s32[1024]{0:T(1024)S(1)} %bitcast.43, bf16[1024,2048]{1,0:T(8,128)(2,1)} %multiply_convert_fusion, f32[]{:T(128)} %constant.11.clone.1), kind=kCustom, calls=%fused_computation.4 | custom fusion | flops 4194304 | bytes 12582916
  138.2 6.0 %convert_element_type.40 = bf16[1024,2048]{1,0:T(8,128)(2,1)} convert(f32[1024,2048]{1,0:T(8,128)} %scatter_custom_fusion.1) | non-fusion elementwise | flops 2097152 | bytes 12582912 | tf_op jit(solution)/shard_map/convert_element_type | solution.py:66
  144.2 0.0 reduce-scatter.2.cloned.1.call-update
  144.3 61.7 %reduce-scatter.2.cloned.1.call-done = bf16[256,2048]{1,0:T(8,128)(2,1)} async-done(((bf16[1024,2048]{1,0:T(8,128)(2,1)}), bf16[256,2048]{1,0:T(8,128)(2,1)}) %reduce-scatter.2.cloned.1.call-update) | async-done | bytes 1048592 | tf_op jit(solution)/shard_map/reduce_scatter | solution.py:65
  (24 shorter events, 0.2 us)
Async XLA Ops:
  6.5 108.1 %copy-start = (bf16[1,768,2048]{2,1,0:T(8,128)(2,1)S(1)}, bf16[1,768,2048]{2,1,0:T(8,128)(2,1)}, u32[]{:S(2)}) copy-start(bf16[1,768,2048]{2,1,0:T(8,128)(2,1)} %param.9) | copy-start | bytes 9437188
  6.5 58.1 %all-gather.2.cloned.1.call-start = ((), (), s32[]{:S(2)}) async-start(), calls=%async_computation.1 | async-start | bytes 5242880 | tf_op jit(solution)/shard_map/all_gather | solution.py:48
  7.3 198.7 %reduce-scatter.2.cloned.1.call-start = ((), (), s32[]{:S(2)}) async-start(), calls=%async_computation.2 | async-start | bytes 5242880 | tf_op jit(solution)/shard_map/reduce_scatter | solution.py:65
Sparse Core Ops, SparseCore 0:
  9.2 55.4 all-gather.1
  144.4 61.5 reduce-scatter.1
where the time goes:
time: 214 us; the launch traced here: 213 us
  waiting for transfers between devices  83.8 us (39%)
  local copies, waits for them, and re-layouts  52.3 us (24%)
  other arithmetic  31.5 us (15%)
  blocking collectives  17.7 us (8%)
  matrix products  13.8 us (6%)
  between operations  13.5 us (6%)
    reduce_scatter x1, waiting for transfers between devices, local(): lax.psum_scatter(partial_out.reshape(groups * tok_rows, width).astype(jnp...  61.7 us
    gather x1, local copies, waits for them, and re-layouts, local(): picked = jnp.take_along_axis(gathered, clipped[:, :, None], axis=1)  38.5 us
    unnamed x9, other arithmetic  21.5 us
    all_gather x1, waiting for transfers between devices, local(): lax.all_gather(tokens, 'expert', axis=0, tiled=True)  21.4 us
    all_gather x1, blocking collectives, local(): lax.all_gather(routes, 'expert', axis=0, tiled=True)  9.77 us
    gather x2, local copies, waits for them, and re-layouts, assign_slots(): slot_weight = jnp.where(is_used, weights[clipped], 0.0)  9.14 us
    dot_general x1, matrix products, expert_block(): projected = jnp.dot(flat_rows, w_first, preferred_element_type=jnp.float32)  8.76 us
    all_gather x1, blocking collectives, local(): lax.all_gather(gate_values, 'expert', axis=0, tiled=True)  7.94 us
  transfers between devices with their start and end apart: 2, of which 2 were waited for; matrix products, arithmetic and copies ran while one was open for 9% of the time, Pallas kernels for 0%

commit v1 on v0

v1 whole, which is shorter than its diff:
```python
import jax
import jax.numpy as jnp
from jax import lax
from jax.experimental import pallas as pl
from jax.experimental.pallas import tpu as pltpu
from jax.sharding import PartitionSpec as P

MESH = pl.DeviceIdType.MESH


def square_kernel(
    routes_ref, gates_ref, tokens_ref, w_in_ref, w_out_ref, out_ref,
    w1, w2, own, buf_x, buf_y, buf_d, comb_own, comb_x, comb_y, comb_d,
    c_own, c_x, c_y, c_d, got_x, got_y, via_y, via_x, hidden,
    local_sem, send_sem, recv_sem,
):
    me = lax.axis_index("expert")
    x_dev = me + 1 - 2 * (me % 2)
    y_dev = (me + 2) % 4
    rows, width = own.shape
    half = rows // 2
    units = w2.shape[0]
    first, second = 0, half
    piece = half // 4

    barrier = pltpu.get_barrier_semaphore()
    for dev in (x_dev, y_dev):
        pl.semaphore_signal(barrier, inc=1, device_id={"expert": dev}, device_id_type=MESH)

    load_w1 = pltpu.make_async_copy(w_in_ref, w1, local_sem.at[0])
    load_w2 = pltpu.make_async_copy(w_out_ref, w2, local_sem.at[1])
    load_own = pltpu.make_async_copy(tokens_ref, own, local_sem.at[2])
    load_own.start()
    load_w1.start()
    load_w2.start()

    experts = lax.broadcasted_iota(jnp.int32, comb_own.shape, 0)
    combined = jnp.zeros(comb_own.shape, jnp.float32)
    for j in range(routes_ref.shape[0]):
        combined += jnp.where(
            experts == routes_ref[j : j + 1, :], gates_ref[j : j + 1, :].astype(jnp.float32), 0.0
        )
    comb_own[...] = combined.astype(jnp.bfloat16)

    pl.semaphore_wait(barrier, 2)

    count = [0]
    sent = []

    def send(src, dst, dev):
        k = count[0]
        count[0] += 1
        copy = pltpu.make_async_remote_copy(
            src_ref=src,
            dst_ref=dst,
            send_sem=send_sem.at[k],
            recv_sem=recv_sem.at[k],
            device_id={"expert": dev},
            device_id_type=MESH,
        )
        copy.start()
        sent.append(copy)
        return copy

    def part(ref, start, size):
        return ref.at[pl.ds(start, size)]

    tok_x0 = send(part(tokens_ref, first, half), part(buf_x, first, half), x_dev)
    tok_y1 = send(part(tokens_ref, second, half), part(buf_y, second, half), y_dev)
    com_x = send(comb_own, comb_x, x_dev)
    com_y = send(comb_own, comb_y, y_dev)
    tok_x1 = send(part(tokens_ref, second, half), part(buf_x, second, half), x_dev)
    tok_y0 = send(part(tokens_ref, first, half), part(buf_y, first, half), y_dev)

    tile = 256

    def compute(src, comb, dst, start):
        def first_step(j, carry):
            cols = pl.multiple_of(j * tile, tile)
            x = src[pl.ds(start, half), :]
            gate = jnp.dot(x, w1[:, pl.ds(cols, tile)], preferred_element_type=jnp.float32)
            up = jnp.dot(x, w1[:, pl.ds(cols + units, tile)], preferred_element_type=jnp.float32)
            hidden[:, pl.ds(cols, tile)] = (gate / (1.0 + jnp.exp(-gate)) * up).astype(jnp.bfloat16)
            return carry

        lax.fori_loop(0, units // tile, first_step, 0)
        pick = (lax.broadcasted_iota(jnp.int32, (comb.shape[0], 128), 0) == me).astype(jnp.bfloat16)
        weight = lax.dot_general(
            comb[:, pl.ds(start, half)], pick, (((0,), (0,)), ((), ())),
            preferred_element_type=jnp.float32,
        )[:, :1]

        def second_step(j, carry):
            cols = pl.multiple_of(j * 512, 512)
            got = jnp.dot(
                hidden[...], w2[:, pl.ds(cols, 512)], preferred_element_type=jnp.float32
            )
            dst[pl.ds(start, half), pl.ds(cols, 512)] = (got * weight).astype(jnp.bfloat16)
            return carry

        lax.fori_loop(0, width // 512, second_step, 0)

    load_own.wait()
    load_w1.wait()
    load_w2.wait()
    compute(own, comb_own, c_own, first)
    compute(own, comb_own, c_own, second)

    com_x.wait_recv()
    com_y.wait_recv()
    com_d = send(comb_x, comb_d, y_dev)
    tok_x0.wait_recv()
    tok_d0 = send(part(buf_x, first, half), part(buf_d, first, half), y_dev)
    tok_y1.wait_recv()
    tok_d1 = send(part(buf_y, second, half), part(buf_d, second, half), x_dev)
    compute(buf_x, comb_x, c_x, first)
    compute(buf_y, comb_y, c_y, second)

    tok_x1.wait_recv()
    compute(buf_x, comb_x, c_x, second)
    straight = []
    straight.append(send(part(c_x, second, half // 2), part(got_x, second, half // 2), x_dev))
    tok_y0.wait_recv()
    compute(buf_y, comb_y, c_y, first)
    straight.append(send(part(c_y, first, half // 2), part(got_y, first, half // 2), y_dev))

    com_d.wait_recv()
    tok_d0.wait_recv()
    compute(buf_d, comb_d, c_d, first)
    hop_y = [
        send(part(c_d, first + i * piece, piece), part(via_y, i * piece, piece), y_dev)
        for i in range(4)
    ]
    tok_d1.wait_recv()
    compute(buf_d, comb_d, c_d, second)
    hop_x = [
        send(part(c_d, second + i * piece, piece), part(via_x, i * piece, piece), x_dev)
        for i in range(4)
    ]
    mid = half // 2
    straight.append(send(part(c_x, second + mid, mid), part(got_x, second + mid, mid), x_dev))
    straight.append(send(part(c_y, first + mid, mid), part(got_y, first + mid, mid), y_dev))

    def add(dst, dst_start, *terms):
        total = terms[0][0][pl.ds(terms[0][1], piece), :].astype(jnp.float32)
        for ref, start in terms[1:]:
            total = total + ref[pl.ds(start, piece), :].astype(jnp.float32)
        dst[pl.ds(dst_start, piece), :] = total.astype(jnp.bfloat16)

    last_x, last_y = [], []
    for i in range(4):
        at0, at1 = first + i * piece, second + i * piece
        hop_y[i].wait_recv()
        add(c_x, at0, (c_x, at0), (via_y, i * piece))
        last_x.append(send(part(c_x, at0, piece), part(got_x, at0, piece), x_dev))
        hop_x[i].wait_recv()
        add(c_y, at1, (c_y, at1), (via_x, i * piece))
        last_y.append(send(part(c_y, at1, piece), part(got_y, at1, piece), y_dev))

    for copy in straight:
        copy.wait_recv()
    for i in range(4):
        at0, at1 = first + i * piece, second + i * piece
        last_x[i].wait_recv()
        add(out_ref, at0, (c_own, at0), (got_x, at0), (got_y, at0))
        last_y[i].wait_recv()
        add(out_ref, at1, (c_own, at1), (got_x, at1), (got_y, at1))
    for copy in sent:
        copy.wait_send()


COPIES = 29


def local_square(tokens, routes, gate_values, weight_in, weight_out):
    rows, width = tokens.shape
    w_first, w_second = weight_in[0], weight_out[0]
    units = w_second.shape[0]
    block = pltpu.VMEM((rows, width), jnp.bfloat16)
    comb = pltpu.VMEM((16, rows), jnp.bfloat16)
    half_block = pltpu.VMEM((rows // 2, width), jnp.bfloat16)
    in_vmem = pl.BlockSpec(memory_space=pltpu.VMEM)
    anywhere = pl.BlockSpec(memory_space=pl.ANY)
    return pl.pallas_call(
        square_kernel,
        out_shape=jax.ShapeDtypeStruct((rows, width), jnp.bfloat16),
        in_specs=[in_vmem, in_vmem, anywhere, anywhere, anywhere],
        out_specs=in_vmem,
        scratch_shapes=[
            pltpu.VMEM(w_first.shape, jnp.bfloat16),
            pltpu.VMEM(w_second.shape, jnp.bfloat16),
            block, block, block, block,
            comb, comb, comb, comb,
            block, block, block, block,
            block, block,
            half_block, half_block,
            pltpu.VMEM((rows // 2, units), jnp.bfloat16),
            pltpu.SemaphoreType.DMA((3,)),
            pltpu.SemaphoreType.DMA((COPIES,)),
            pltpu.SemaphoreType.DMA((COPIES,)),
        ],
        compiler_params=pltpu.CompilerParams(
            collective_id=0, has_side_effects=True, vmem_limit_bytes=60 * 1024 * 1024
        ),
        cost_estimate=pl.CostEstimate(
            flops=4 * rows * width * units * 6, bytes_accessed=16 << 20, transcendentals=0
        ),
    )(routes.T, gate_values.T, tokens, w_first, w_second)


def local_dense(tokens, routes, gate_values, weight_in, weight_out):
    my_expert = lax.axis_index("expert")
    w_first, w_second = weight_in[0], weight_out[0]
    units = w_second.shape[0]
    experts = jnp.arange(lax.axis_size("expert"), dtype=jnp.int32)[None, None, :]
    matched = routes[:, :, None] == experts
    combine = jnp.sum(jnp.where(matched, gate_values.astype(jnp.float32)[:, :, None], 0.0), axis=1)
    gathered = lax.all_gather(tokens, "expert", axis=0, tiled=True)
    combine = lax.all_gather(combine, "expert", axis=0, tiled=True)
    mine = (experts[0] == my_expert).astype(jnp.float32)
    weight = jnp.sum(combine * mine, axis=1)
    projected = jnp.dot(gathered, w_first, preferred_element_type=jnp.float32)
    hidden = (jax.nn.silu(projected[:, :units]) * projected[:, units:]).astype(jnp.bfloat16)
    expert_out = jnp.dot(hidden, w_second, preferred_element_type=jnp.float32)
    contribution = (expert_out * weight[:, None]).astype(jnp.bfloat16)
    return lax.psum_scatter(contribution, "expert", scatter_dimension=0, tiled=True)


def solution(mesh):
    in_specs = (
        P(("dp", "expert"), None),
        P(("dp", "expert"), None),
        P(("dp", "expert"), None),
        P("expert", None, None),
        P("expert", None, None),
    )
    out_specs = P(("dp", "expert"), None)
    body = local_square if mesh.shape["expert"] == 4 else local_dense
    return jax.shard_map(body, mesh=mesh, in_specs=in_specs, out_specs=out_specs, check_vma=False)
```

time: 214 us -> 77.9 us (0.36)
  waiting for transfers between devices: 83.8 us -> 0 us
  Pallas kernels: 0 us -> 75.4 us
  local copies, waits for them, and re-layouts: 52.3 us -> 2.3 us
  other arithmetic: 31.5 us -> 0 us
  blocking collectives: 17.7 us -> 0 us
  matrix products: 13.8 us -> 0 us
  between operations: 13.5 us -> 0.01 us
    pallas_call x0 -> x1, Pallas kernels: none -> 75.4 us  [local_square(): pl.pallas_call(square_kernel, out_shape=jax.ShapeDtypeStruct((rows, width...]
    reduce_scatter x1 -> x0, waiting for transfers between devices: 61.7 us -> none  [local(): lax.psum_scatter(partial_out.reshape(groups * tok_rows, width).astype(jnp...]
    gather x3 -> x0, local copies, waits for them, and re-layouts: 47.7 us -> none  [the longest x1 38.5 us: local(): picked = jnp.take_along_axis(gathered, clipped[:, :, None], axis=1)]
    unnamed x9 -> x0, other arithmetic: 21.5 us -> none
    all_gather x1 -> x0, waiting for transfers between devices: 21.4 us -> none  [local(): lax.all_gather(tokens, 'expert', axis=0, tiled=True)]
    all_gather x2 -> x0, blocking collectives: 17.7 us -> none  [the longest x1 9.77 us: local(): lax.all_gather(routes, 'expert', axis=0, tiled=True)]
    dot_general x2 -> x0, matrix products: 13.8 us -> none  [the longest x1 8.76 us: expert_block(): projected = jnp.dot(flat_rows, w_first, preferred_element_type=jnp.float32)]
    convert_element_type x2 -> x0, other arithmetic: 6.01 us -> none  [the longest x1 6.01 us: local(): partial_out.reshape(groups * tok_rows, width).astype(jnp.bfloat16)]
  transfers between devices with their start and end apart: 2 -> 0, of which waited for: 2 -> 0; matrix products, arithmetic and copies ran while one was open for 9% -> 0% of each run, Pallas kernels for 0% -> 0%
where the time goes in v1:
time: 77.9 us; the launch traced here: 77.7 us
  Pallas kernels  75.4 us (97%)
  local copies, waits for them, and re-layouts  2.3 us (3%)
    pallas_call x1, Pallas kernels, local_square(): pl.pallas_call(square_kernel, out_shape=jax.ShapeDtypeStruct((rows, width...  75.4 us
    unnamed x1, local copies, waits for them, and re-layouts  2.3 us

profile of v1, /device:TPU:0, one launch (start us, length us, event | category | flops | bytes accessed | tf_op | source)
XLA Modules:
  0.0 77.7 jit_solution(3790321517573635126)
XLA Ops:
  0.0 75.4 %shard_map.55 = bf16[256,2048]{1,0:T(8,128)(2,1)} custom-call(s32[2,256]{1,0:T(2,128)} %bitcast.6, bf16[2,256]{1,0:T(2,128)(2,1)} %bitcast.7, bf16[256,2048]{1,0:T(8,128)(2,1)} %tokens_ref.1, bf16[2048,1536]{1,0:T(8,128)(2,1)} %bitcast.4, bf16[768,2048]{1,0:T(8,128)(2,1)} %bitcast.5), custom_call_target="tpu_custom_call" | custom-call | flops 9663676416 | bytes 16777216 | tf_op jit(solution)/shard_map/pallas_call | solution.py:184
  75.4 2.3 %copy.7 = bf16[256,2048]{1,0:T(8,128)(2,1)} copy(bf16[256,2048]{1,0:T(8,128)(2,1)} %shard_map.55) | data formatting | bytes 2097152

commit v2 on v1

--- a/solution.py
+++ b/solution.py
@@ -9,8 +9,8 @@
 
 
 def square_kernel(
-    routes_ref, gates_ref, tokens_ref, w_in_ref, w_out_ref, out_ref,
-    w1, w2, own, buf_x, buf_y, buf_d, comb_own, comb_x, comb_y, comb_d,
+    routes_hbm, gates_hbm, tokens_ref, w_in_ref, w_out_ref, out_ref,
+    routes_ref, gates_ref, w1, w2, own, buf_x, buf_y, buf_d, comb_own, comb_x, comb_y, comb_d,
     c_own, c_x, c_y, c_d, got_x, got_y, via_y, via_x, hidden,
     local_sem, send_sem, recv_sem,
 ):
@@ -30,18 +30,10 @@
     load_w1 = pltpu.make_async_copy(w_in_ref, w1, local_sem.at[0])
     load_w2 = pltpu.make_async_copy(w_out_ref, w2, local_sem.at[1])
     load_own = pltpu.make_async_copy(tokens_ref, own, local_sem.at[2])
-    load_own.start()
-    load_w1.start()
-    load_w2.start()
-
-    experts = lax.broadcasted_iota(jnp.int32, comb_own.shape, 0)
-    combined = jnp.zeros(comb_own.shape, jnp.float32)
-    for j in range(routes_ref.shape[0]):
-        combined += jnp.where(
-            experts == routes_ref[j : j + 1, :], gates_ref[j : j + 1, :].astype(jnp.float32), 0.0
-        )
-    comb_own[...] = combined.astype(jnp.bfloat16)
-
+    load_routes = pltpu.make_async_copy(routes_hbm, routes_ref, local_sem.at[3])
+    load_gates = pltpu.make_async_copy(gates_hbm, gates_ref, local_sem.at[4])
+    load_routes.start()
+    load_gates.start()
     pl.semaphore_wait(barrier, 2)
 
     count = [0]
@@ -67,10 +59,21 @@
 
     tok_x0 = send(part(tokens_ref, first, half), part(buf_x, first, half), x_dev)
     tok_y1 = send(part(tokens_ref, second, half), part(buf_y, second, half), y_dev)
+    load_own.start()
+    load_w1.start()
+    load_w2.start()
+
+    load_routes.wait()
+    load_gates.wait()
+    experts = lax.broadcasted_iota(jnp.int32, comb_own.shape, 0)
+    combined = jnp.zeros(comb_own.shape, jnp.float32)
+    for j in range(routes_ref.shape[0]):
+        combined += jnp.where(
+            experts == routes_ref[j : j + 1, :], gates_ref[j : j + 1, :].astype(jnp.float32), 0.0
+        )
+    comb_own[...] = combined.astype(jnp.bfloat16)
     com_x = send(comb_own, comb_x, x_dev)
     com_y = send(comb_own, comb_y, y_dev)
-    tok_x1 = send(part(tokens_ref, second, half), part(buf_x, second, half), x_dev)
-    tok_y0 = send(part(tokens_ref, first, half), part(buf_y, first, half), y_dev)
 
     tile = 256
 
@@ -104,6 +107,8 @@
     load_w1.wait()
     load_w2.wait()
     compute(own, comb_own, c_own, first)
+    tok_x1 = send(part(tokens_ref, second, half), part(buf_x, second, half), x_dev)
+    tok_y0 = send(part(tokens_ref, first, half), part(buf_y, first, half), y_dev)
     compute(own, comb_own, c_own, second)
 
     com_x.wait_recv()
@@ -117,29 +122,25 @@
     compute(buf_y, comb_y, c_y, second)
 
     tok_x1.wait_recv()
+    straight_x = send(part(c_x, first, half), part(got_x, first, half), x_dev)
+    tok_y0.wait_recv()
+    straight_y = send(part(c_y, second, half), part(got_y, second, half), y_dev)
     compute(buf_x, comb_x, c_x, second)
-    straight = []
-    straight.append(send(part(c_x, second, half // 2), part(got_x, second, half // 2), x_dev))
-    tok_y0.wait_recv()
     compute(buf_y, comb_y, c_y, first)
-    straight.append(send(part(c_y, first, half // 2), part(got_y, first, half // 2), y_dev))
 
     com_d.wait_recv()
     tok_d0.wait_recv()
     compute(buf_d, comb_d, c_d, first)
-    hop_y = [
-        send(part(c_d, first + i * piece, piece), part(via_y, i * piece, piece), y_dev)
+    hop_x = [
+        send(part(c_d, first + i * piece, piece), part(via_x, i * piece, piece), x_dev)
         for i in range(4)
     ]
     tok_d1.wait_recv()
     compute(buf_d, comb_d, c_d, second)
-    hop_x = [
-        send(part(c_d, second + i * piece, piece), part(via_x, i * piece, piece), x_dev)
+    hop_y = [
+        send(part(c_d, second + i * piece, piece), part(via_y, i * piece, piece), y_dev)
         for i in range(4)
     ]
-    mid = half // 2
-    straight.append(send(part(c_x, second + mid, mid), part(got_x, second + mid, mid), x_dev))
-    straight.append(send(part(c_y, first + mid, mid), part(got_y, first + mid, mid), y_dev))
 
     def add(dst, dst_start, *terms):
         total = terms[0][0][pl.ds(terms[0][1], piece), :].astype(jnp.float32)
@@ -150,26 +151,26 @@
     last_x, last_y = [], []
     for i in range(4):
         at0, at1 = first + i * piece, second + i * piece
+        hop_x[i].wait_recv()
+        add(c_y, at0, (c_y, at0), (via_x, i * piece))
+        last_y.append(send(part(c_y, at0, piece), part(got_y, at0, piece), y_dev))
         hop_y[i].wait_recv()
-        add(c_x, at0, (c_x, at0), (via_y, i * piece))
-        last_x.append(send(part(c_x, at0, piece), part(got_x, at0, piece), x_dev))
-        hop_x[i].wait_recv()
-        add(c_y, at1, (c_y, at1), (via_x, i * piece))
-        last_y.append(send(part(c_y, at1, piece), part(got_y, at1, piece), y_dev))
-
-    for copy in straight:
-        copy.wait_recv()
+        add(c_x, at1, (c_x, at1), (via_y, i * piece))
+        last_x.append(send(part(c_x, at1, piece), part(got_x, at1, piece), x_dev))
+
+    straight_x.wait_recv()
+    straight_y.wait_recv()
     for i in range(4):
         at0, at1 = first + i * piece, second + i * piece
+        last_y[i].wait_recv()
+        add(out_ref, at0, (c_own, at0), (got_x, at0), (got_y, at0))
         last_x[i].wait_recv()
-        add(out_ref, at0, (c_own, at0), (got_x, at0), (got_y, at0))
-        last_y[i].wait_recv()
         add(out_ref, at1, (c_own, at1), (got_x, at1), (got_y, at1))
     for copy in sent:
         copy.wait_send()
 
 
-COPIES = 29
+COPIES = 27
 
 
 def local_square(tokens, routes, gate_values, weight_in, weight_out):
@@ -184,9 +185,11 @@
     return pl.pallas_call(
         square_kernel,
         out_shape=jax.ShapeDtypeStruct((rows, width), jnp.bfloat16),
-        in_specs=[in_vmem, in_vmem, anywhere, anywhere, anywhere],
+        in_specs=[anywhere, anywhere, anywhere, anywhere, anywhere],
         out_specs=in_vmem,
         scratch_shapes=[
+            pltpu.VMEM((routes.shape[1], rows), jnp.int32),
+            pltpu.VMEM((routes.shape[1], rows), jnp.bfloat16),
             pltpu.VMEM(w_first.shape, jnp.bfloat16),
             pltpu.VMEM(w_second.shape, jnp.bfloat16),
             block, block, block, block,
@@ -195,7 +198,7 @@
             block, block,
             half_block, half_block,
             pltpu.VMEM((rows // 2, units), jnp.bfloat16),
-            pltpu.SemaphoreType.DMA((3,)),
+            pltpu.SemaphoreType.DMA((5,)),
             pltpu.SemaphoreType.DMA((COPIES,)),
             pltpu.SemaphoreType.DMA((COPIES,)),
         ],

time: 77.9 us -> 77 us (0.988)
  Pallas kernels: 75.4 us -> 74.5 us
    pallas_call x1, Pallas kernels: 75.4 us -> 74.5 us  [local_square(): pl.pallas_call(square_kernel, out_shape=jax.ShapeDtypeStruct((rows, width...]
where the time goes in v2:
time: 77 us; the launch traced here: 76.8 us
  Pallas kernels  74.5 us (97%)
  local copies, waits for them, and re-layouts  2.3 us (3%)
    pallas_call x1, Pallas kernels, local_square(): pl.pallas_call(square_kernel, out_shape=jax.ShapeDtypeStruct((rows, width...  74.5 us
    unnamed x1, local copies, waits for them, and re-layouts  2.3 us

profile of v2, /device:TPU:0, one launch (start us, length us, event | category | flops | bytes accessed | tf_op | source)
XLA Modules:
  0.0 76.8 jit_solution(12099949993301385798)
XLA Ops:
  0.0 74.5 %shard_map.55 = bf16[256,2048]{1,0:T(8,128)(2,1)} custom-call(s32[2,256]{1,0:T(2,128)} %bitcast.6, bf16[2,256]{1,0:T(2,128)(2,1)} %bitcast.7, bf16[256,2048]{1,0:T(8,128)(2,1)} %tokens_ref.1, bf16[2048,1536]{1,0:T(8,128)(2,1)} %bitcast.4, bf16[768,2048]{1,0:T(8,128)(2,1)} %bitcast.5), custom_call_target="tpu_custom_call" | custom-call | flops 9663676416 | bytes 16777216 | tf_op jit(solution)/shard_map/pallas_call | solution.py:185
  74.5 2.3 %copy.7 = bf16[256,2048]{1,0:T(8,128)(2,1)} copy(bf16[256,2048]{1,0:T(8,128)(2,1)} %shard_map.55) | data formatting | bytes 2097152

commit v3 on v2

--- a/solution.py
+++ b/solution.py
@@ -203,7 +203,7 @@
             pltpu.SemaphoreType.DMA((COPIES,)),
         ],
         compiler_params=pltpu.CompilerParams(
-            collective_id=0, has_side_effects=True, vmem_limit_bytes=60 * 1024 * 1024
+            collective_id=0, has_side_effects=True, vmem_limit_bytes=52 * 1024 * 1024
         ),
         cost_estimate=pl.CostEstimate(
             flops=4 * rows * width * units * 6, bytes_accessed=16 << 20, transcendentals=0

time: 77 us -> 76 us (0.987)
  Pallas kernels: 74.5 us -> 73.5 us
    pallas_call x1, Pallas kernels: 74.5 us -> 73.5 us  [local_square(): pl.pallas_call(square_kernel, out_shape=jax.ShapeDtypeStruct((rows, width...]
    unnamed x1 -> x5, local copies, waits for them, and re-layouts: 2.3 us -> 2.33 us
where the time goes in v3:
time: 76 us; the launch traced here: 75.8 us
  Pallas kernels  73.5 us (97%)
  local copies, waits for them, and re-layouts  2.33 us (3%)
    pallas_call x1, Pallas kernels, local_square(): pl.pallas_call(square_kernel, out_shape=jax.ShapeDtypeStruct((rows, width...  73.5 us
    unnamed x5, local copies, waits for them, and re-layouts  2.33 us

profile of v3, /device:TPU:0, one launch (start us, length us, event | category | flops | bytes accessed | tf_op | source)
XLA Modules:
  0.0 75.8 jit_solution(6337918509123894731)
XLA Ops:
  0.0 0.0 copy-start
  0.0 0.7 copy-done
  0.7 0.0 copy-start.1
  0.7 0.7 copy-done.1
  1.4 73.5 %shard_map.55 = bf16[256,2048]{1,0:T(8,128)(2,1)S(1)} custom-call(s32[2,256]{1,0:T(2,128)S(1)} %bitcast.4, bf16[2,256]{1,0:T(2,128)(2,1)S(1)} %bitcast.5, bf16[256,2048]{1,0:T(8,128)(2,1)} %tokens_ref.1, bf16[2048,1536]{1,0:T(8,128)(2,1)} %bitcast.6, bf16[768,2048]{1,0:T(8,128)(2,1)} %bitcast.7), custom_call_target="tpu_custom_call" | custom-call | flops 9663676416 | bytes 16777216 | tf_op jit(solution)/shard_map/pallas_call | solution.py:185
  74.9 1.0 %copy.7 = bf16[256,2048]{1,0:T(8,128)(2,1)} copy(bf16[256,2048]{1,0:T(8,128)(2,1)S(1)} %shard_map.55) | data formatting | bytes 2097152
Async XLA Ops:
  0.0 0.7 copy-start
  0.7 0.7 copy-start.1
